TPU v7x, 256 devices: a whole 4x4x8 slice. The times are simulated.
256 devices in a mesh: ent: 32 (over y, x, core), rel: 8 (over z).
Axes of the slice: x: 4, y: 4, z: 8, core: 2. Of those that a mesh axis runs over, the one named last changes fastest.
Arguments:
- tile_vals: bfloat16 [32, 8, 64, 128, 128], P('ent', 'rel'), may hold values from -192 to 192
- tile_row: int32 [32, 8, 64], P('ent', 'rel'), may hold values from 0 to 3
- tile_rel: int32 [32, 8, 64], P('ent', 'rel'), may hold values from 0 to 1
- tile_src: int32 [32, 8, 64], P('ent', 'rel'), may hold values from 0 to 31
- needed: int32 [32, 8, 32, 1], P('ent', 'rel'), may hold values from 0 to 3
- factors: bfloat16 [16384, 256], P('ent'), may hold values from -6 to 6
- cores: bfloat16 [16, 256, 256], P('rel'), may hold values from -0.5 to 1.5
- basis: float32 [256, 256], replicated, may hold values from -1 to 1
- spectrum: float32 [256], replicated, may hold values from 100 to 1000
Outputs:
- new_factors: bfloat16 [16384, 256], P('ent')
- new_cores: float32 [16, 256, 256], P('rel')
Inputs may be any that keep to these rules, and one draw needn't show every extreme that they name: tile_src names the owner whose single requested block (slot 0 of `needed`) gives the tile's columns. `needed`: every request slot names a block.
All inputs are finite; a program needn't handle non-finite values.
Results may differ from a plain program's by a relative error of at most 0.0081.
Values may be sent and summed in bfloat16 or wider, within the bound.
A program may use at most 64 MiB of HBM per device.

v0:
```python
import jax
import jax.numpy as jnp
from jax import lax
from jax.sharding import PartitionSpec as P

ridge_shift = 1.0


def shards(tile_vals, tile_row, tile_rel, tile_src, needed, factors, cores, basis, spectrum):
    precise = lax.Precision.HIGHEST
    tile_data = tile_vals[0, 0]
    tile_rows = tile_row[0, 0]
    tile_rels = tile_rel[0, 0]
    sources = tile_src[0, 0]
    asked_rows = needed[0, 0]
    count_ent, slot_count = asked_rows.shape
    tile_edge = tile_data.shape[1]
    rank_width = factors.shape[1]
    rel_local = cores.shape[0]
    row_blocks = factors.shape[0] // tile_edge
    slot_total = count_ent * slot_count
    requests = lax.all_to_all(asked_rows, "ent", split_axis=0, concat_axis=0, tiled=True)

    def neighbour(slab_rows):
        whole_table = lax.all_gather(slab_rows, "ent", axis=0, tiled=True).reshape(
            count_ent, row_blocks, tile_edge, rank_width
        )
        fetched = whole_table[jnp.arange(count_ent)[:, None], asked_rows]
        return fetched.reshape(slot_total, tile_edge, rank_width)[sources]

    def grouped(part_data, key_ids, group_count):
        onehot = (key_ids[:, None] == jnp.arange(group_count, dtype=jnp.int32)[None, :]).astype(
            jnp.bfloat16
        )
        flat_part = part_data.reshape(part_data.shape[0], tile_edge * rank_width)
        return jnp.einsum(
            "tg,tx->gx", onehot, flat_part, preferred_element_type=jnp.float32
        ).astype(jnp.bfloat16)

    gathered_old = neighbour(factors)
    left_part = jnp.einsum(
        "tab,tbr->tar", tile_data, gathered_old, preferred_element_type=jnp.float32
    ).astype(jnp.bfloat16)
    forward = grouped(
        left_part, tile_rels * row_blocks + tile_rows, rel_local * row_blocks
    ).reshape(rel_local, row_blocks, tile_edge, rank_width)
    forward_term = jnp.einsum(
        "kbar,ksr->bas", forward, cores, preferred_element_type=jnp.float32
    ).reshape(-1, rank_width)
    own_blocks = factors.reshape(row_blocks, tile_edge, rank_width)
    right_part = jnp.einsum(
        "tab,tar->tbr", tile_data, own_blocks[tile_rows], preferred_element_type=jnp.float32
    ).astype(jnp.bfloat16)
    backward = grouped(right_part, sources * rel_local + tile_rels, slot_total * rel_local).reshape(
        slot_total, rel_local, tile_edge, rank_width
    )
    backward_term = jnp.einsum(
        "skbr,krq->sbq", backward, cores, preferred_element_type=jnp.float32
    ).reshape(count_ent, slot_count, tile_edge, rank_width)
    returned = lax.all_to_all(backward_term, "ent", split_axis=0, concat_axis=0, tiled=True)
    landing = (
        requests.reshape(1, slot_total) == jnp.arange(row_blocks, dtype=jnp.int32)[:, None]
    ).astype(jnp.float32)
    landed = jnp.dot(
        landing,
        returned.reshape(slot_total, tile_edge * rank_width),
        precision=precise,
        preferred_element_type=jnp.float32,
    ).reshape(-1, rank_width)
    gram_total = lax.psum(
        jnp.einsum("ar,as->rs", factors, factors, preferred_element_type=jnp.float32), "ent"
    )
    core_f32 = cores.astype(jnp.float32)
    system_part = jnp.einsum("kab,bc,kdc->ad", core_f32, gram_total, core_f32, precision=precise)
    system_part = system_part + jnp.einsum(
        "kba,bc,kcd->ad", core_f32, gram_total, core_f32, precision=precise
    )
    numerator, system = lax.psum((forward_term + landed, system_part), "rel")
    system = system + ridge_shift * jnp.eye(rank_width, dtype=jnp.float32)
    factor_low = jnp.linalg.cholesky(system)
    new_factors = jax.scipy.linalg.cho_solve((factor_low, True), numerator.T).T.astype(jnp.bfloat16)
    gathered_new = neighbour(new_factors)
    latest = jnp.einsum(
        "tab,tbr->tar", tile_data, gathered_new, preferred_element_type=jnp.float32
    ).astype(jnp.bfloat16)
    summed = grouped(latest, tile_rels * row_blocks + tile_rows, rel_local * row_blocks).reshape(
        rel_local, row_blocks, tile_edge, rank_width
    )
    core_part = jnp.einsum(
        "bar,kbas->krs",
        new_factors.reshape(row_blocks, tile_edge, rank_width),
        summed,
        preferred_element_type=jnp.float32,
    )
    weights = 1.0 / (spectrum[:, None] * spectrum[None, :] + ridge_shift)
    totals = lax.psum(core_part, "ent")
    rotated = jnp.einsum("ri,krs,sj->kij", basis, totals, basis, precision=precise)
    new_cores = jnp.einsum(
        "ir,krs,js->kij", basis, weights[None] * rotated, basis, precision=precise
    )
    return (new_factors, new_cores)


def solution(mesh):
    in_specs = (
        P("ent", "rel", None, None, None),
        P("ent", "rel", None),
        P("ent", "rel", None),
        P("ent", "rel", None),
        P("ent", "rel", None, None),
        P("ent", None),
        P("rel", None, None),
        P(),
        P(),
    )
    out_specs = (P("ent", None), P("rel", None, None))
    return jax.shard_map(shards, mesh=mesh, in_specs=in_specs, out_specs=out_specs, check_vma=False)
```

profile of v0, /device:TPU:1, one launch (start us, length us, event | category | flops | bytes accessed | tf_op | source)
XLA Modules:
  0.0 606.0 jit_solution(6752421999504624473)
XLA Ops:
  7.2 2.2 fusion.37
  9.5 0.7 all-gather.3.cloned.1.call-update
  10.2 1.3 copy.58
  11.5 8.6 %all-to-all-start = ((s32[32,1,1]{2,1,0:T(1,128)}), s32[32,1,1]{2,1,0:T(1,128)S(1)}, u32[]{:S(2)}, u32[]{:S(2)}) async-start(s32[32,1,1]{2,1,0:T(1,128)} %copy.58), calls=%async_computation | async-start | bytes 32768 | tf_op jit(solution)/shard_map/all_to_all | solution.py:22
  20.1 0.7 fusion.34
  20.8 2.7 gather_fusion.2
  23.5 5.5 convert_bitcast_fusion.1
  29.0 6.8 %copy.96 = bf16[8,8,128,256]{3,1,2,0:T(8,128)(2,1)} copy(bf16[8,8,128,256]{2,3,1,0:T(8,128)(2,1)} %bitcast.176) | data formatting | bytes 8388608
  35.9 3.6 convolution_convert_fusion
  39.5 1.1 copy.97
  40.6 3.2 convolution_bitcast_fusion
  43.8 7.6 %all-to-all-start.1 = ((f32[32,1,128,256]{3,2,1,0:T(8,128)}), f32[32,1,128,256]{3,2,1,0:T(8,128)}, u32[]{:S(2)}, u32[]{:S(2)}) async-start(f32[32,1,128,256]{3,2,1,0:T(8,128)} %convolution_bitcast_fusion), calls=%async_computation.1 | async-start | bytes 8388608 | tf_op jit(solution)/shard_map/all_to_all | solution.py:60
  51.3 0.5 all-reduce.10.cloned.1.call-start
  51.9 0.7 reduce.12
  52.6 100.5 %all-reduce.6.cloned.1.call-done = f32[256,256]{1,0:T(8,128)} async-done(((f32[256,256]{1,0:T(8,128)}), f32[256,256]{1,0:T(8,128)}) %all-reduce.6.cloned.1.call-update) | async-done | bytes 262160 | tf_op jit(solution)/shard_map/psum | solution.py:70
  153.1 1.4 fusion.17
  154.6 0.5 convolution_bitcast_fusion.3
  155.0 1.3 fusion.19
  156.4 1.2 fusion.5
  157.5 4.6 copy.98
  162.2 1.5 fusion.31
  163.7 0.4 reshape.241
  164.1 50.2 %all-gather.3.cloned.1.call-done = bf16[16384,256]{1,0:T(8,128)(2,1)} async-done(((bf16[512,256]{1,0:T(8,128)(2,1)}), bf16[16384,256]{1,0:T(8,128)(2,1)}) %all-gather.3.cloned.1.call-update) | async-done | bytes 8388624 | tf_op jit(solution)/shard_map/all_gather | solution.py:25
  214.2 5.4 gather_fusion
  219.7 4.4 gather_fusion.1
  224.0 5.5 convert_bitcast_fusion.2
  229.5 6.8 %copy.94 = bf16[8,8,128,256]{3,1,2,0:T(8,128)(2,1)} copy(bf16[8,8,128,256]{2,3,1,0:T(8,128)(2,1)} %bitcast.177) | data formatting | bytes 8388608
  236.3 2.9 convolution_convert_fusion.2
  239.4 1.1 fusion.4
  240.8 69.7 %all-reduce.10.cloned.1.call-done = (f32[256,512]{0,1:T(8,128)}, f32[256,256]{0,1:T(8,128)}) async-done(((f32[256,512]{0,1:T(8,128)}, f32[256,256]{0,1:T(8,128)}), (f32[256,512]{0,1:T(8,128)}, f32[256,256]{0,1:T(8,128)})) %all-reduce.10.cloned.1.call-update) | async-done | bytes 786448 | tf_op jit(solution)/shard_map/psum | solution.py:78
  310.5 1.0 convert_add_fusion
  311.6 1.0 fusion.16
  312.7 11.7 %cholesky.50 = f32[128,128]{1,0:T(8,128)S(1)} custom-call(f32[128,128]{1,0:T(8,128)S(1)} %cholesky.118), custom_call_target="Cholesky" | custom-call | tf_op jit(solution)/shard_map/jit(cholesky)/cholesky | solution.py:80
  324.4 9.8 %custom-call.18 = f32[1,128,128]{1,2,0:T(8,128)S(1)} custom-call(f32[1,128,128]{2,1,0:T(8,128)S(1)} %get-tuple-element.33), custom_call_target="InvertDiagBlocksLowerTriangular" | custom-call | tf_op jit(solution)/shard_map/jit(cholesky)/cholesky | solution.py:80
  334.5 0.3 convolution_subtract_fusion.2
  334.7 11.7 %cholesky.105 = f32[128,128]{1,0:T(8,128)S(1)} custom-call(f32[128,128]{1,0:T(8,128)S(1)} %convolution_subtract_fusion.2), custom_call_target="Cholesky" | custom-call | tf_op jit(solution)/shard_map/jit(cholesky)/cholesky | solution.py:80
  346.5 0.6 compare_reduce_fusion
  348.5 4.2 while.1
  348.7 0.6 fusion.70
  349.3 1.4 bitcast_dynamic-update-slice_fusion.2
  350.7 0.6 fusion.70
  351.3 1.4 bitcast_dynamic-update-slice_fusion.2
  352.7 19.7 %custom-call.19 = f32[2,128,128]{1,2,0:T(8,128)S(1)} custom-call(f32[2,128,128]{2,1,0:T(8,128)S(1)} %get-tuple-element.9), custom_call_target="InvertDiagBlocksLowerTriangular" | custom-call | tf_op jit(solution)/shard_map/jit(_cho_solve)/triangular_solve | solution.py:81
  372.4 0.4 fusion.6
  372.8 0.6 convolution_subtract_fusion.1
  373.4 0.4 fusion.25
  373.9 0.4 fusion.36
  374.2 0.4 convolution_subtract_fusion
  374.7 0.4 convolution_convert_fusion.3
  375.0 0.7 maximum_bitcast_fusion
  375.8 1.1 copy.71
  376.9 66.5 %all-gather.5.cloned.1.call-done = bf16[16384,256]{0,1:T(8,128)(2,1)} async-done(((bf16[512,256]{0,1:T(8,128)(2,1)}), bf16[16384,256]{0,1:T(8,128)(2,1)}) %all-gather.5.cloned.1.call-update) | async-done | bytes 8388624 | tf_op jit(solution)/shard_map/all_gather | solution.py:25
  443.4 12.0 %copy.92 = bf16[16384,256]{1,0:T(8,128)(2,1)} copy(bf16[16384,256]{0,1:T(8,128)(2,1)} %all-gather.5.cloned.1.call-done) | data formatting | bytes 16777216 | tf_op jit(solution)/shard_map/reshape | solution.py:25
  455.4 5.4 gather_fusion.3
  460.8 4.4 gather_fusion.4
  465.2 5.5 convert_bitcast_fusion
  470.7 6.8 %copy.99 = bf16[8,8,128,256]{3,1,2,0:T(8,128)(2,1)} copy(bf16[8,8,128,256]{2,3,1,0:T(8,128)(2,1)} %bitcast.178) | data formatting | bytes 8388608
  477.5 3.0 convolution_convert_fusion.1
  480.6 1.1 convolution_bitcast_fusion.1
  481.9 112.9 %all-reduce.8.cloned.1.call-done = f32[2,256,256]{1,2,0:T(8,128)} async-done(((f32[2,256,256]{1,2,0:T(8,128)}), f32[2,256,256]{1,2,0:T(8,128)}) %all-reduce.8.cloned.1.call-update) | async-done | bytes 524304 | tf_op jit(solution)/shard_map/psum | solution.py:96
  594.9 1.7 fusion.13
  596.6 0.6 convolution_multiply_fusion
  597.2 0.6 fusion.10
  597.8 1.4 fusion.8
  (55 shorter events, 1.4 us)
Async XLA Ops:
  7.2 16.4 %copy-start = (bf16[1,1,64,128,128]{4,3,2,1,0:T(8,128)(2,1)S(1)}, bf16[1,1,64,128,128]{4,3,2,1,0:T(8,128)(2,1)}, u32[]{:S(2)}) copy-start(bf16[1,1,64,128,128]{4,3,2,1,0:T(8,128)(2,1)} %param.9) | copy-start | bytes 6291460
  7.2 13.6 %copy-start.1 = (bf16[512,256]{1,0:T(8,128)(2,1)S(1)}, bf16[512,256]{1,0:T(8,128)(2,1)}, u32[]{:S(2)}) copy-start(bf16[512,256]{1,0:T(8,128)(2,1)} %param.14) | copy-start | bytes 786436
  7.2 145.9 %all-reduce.6.cloned.1.call-start = ((), (), s32[]{:S(2)}) async-start(), calls=%async_computation.2 | async-start | bytes 524288 | tf_op jit(solution)/shard_map/psum | solution.py:70
  9.4 204.8 %all-gather.3.cloned.1.call-start = ((), (), s32[]{:S(2)}) async-start(), calls=%async_computation.3 | async-start | bytes 8650752 | tf_op jit(solution)/shard_map/all_gather | solution.py:25
  11.5 32.2 %all-to-all-start = ((s32[32,1,1]{2,1,0:T(1,128)}), s32[32,1,1]{2,1,0:T(1,128)S(1)}, u32[]{:S(2)}, u32[]{:S(2)}) async-start(s32[32,1,1]{2,1,0:T(1,128)} %copy.58), calls=%async_computation | async-start | bytes 32768 | tf_op jit(solution)/shard_map/all_to_all | solution.py:22
  29.0 6.8 %copy-start.7 = (s32[1,1,64]{2,1,0:T(1,128)S(1)}, s32[1,1,64]{2,1,0:T(1,128)}, u32[]{:S(2)}) copy-start(s32[1,1,64]{2,1,0:T(1,128)} %param.10) | copy-start | bytes 772
  29.0 6.8 %copy-start.8 = (s32[1,1,64]{2,1,0:T(1,128)S(1)}, s32[1,1,64]{2,1,0:T(1,128)}, u32[]{:S(2)}) copy-start(s32[1,1,64]{2,1,0:T(1,128)} %param.11) | copy-start | bytes 772
  29.0 6.8 %copy-start.10 = (s32[1,1,64]{2,1,0:T(1,128)S(1)}, s32[1,1,64]{2,1,0:T(1,128)}, u32[]{:S(2)}) copy-start(s32[1,1,64]{2,1,0:T(1,128)} %param.12) | copy-start | bytes 772
  39.4 1.1 copy-start.2
  43.8 8.1 %copy-start.9 = (s32[1,1,32,1]{2,3,1,0:T(1,128)S(1)}, s32[1,1,32,1]{2,3,1,0:T(1,128)}, u32[]{:S(2)}) copy-start(s32[1,1,32,1]{2,3,1,0:T(1,128)} %param.13) | copy-start | bytes 388
  43.8 113.8 %all-to-all-start.1 = ((f32[32,1,128,256]{3,2,1,0:T(8,128)}), f32[32,1,128,256]{3,2,1,0:T(8,128)}, u32[]{:S(2)}, u32[]{:S(2)}) async-start(f32[32,1,128,256]{3,2,1,0:T(8,128)} %convolution_bitcast_fusion), calls=%async_computation.1 | async-start | bytes 8388608 | tf_op jit(solution)/shard_map/all_to_all | solution.py:60
  51.3 259.1 %all-reduce.10.cloned.1.call-start = ((), (), s32[]{:S(2)}) async-start(), calls=%async_computation.6 | async-start | bytes 1572864 | tf_op jit(solution)/shard_map/psum | solution.py:78
  240.5 202.9 %all-gather.5.cloned.1.call-start = ((), (), s32[]{:S(2)}) async-start(), calls=%async_computation.4 | async-start | bytes 8650752 | tf_op jit(solution)/shard_map/all_gather | solution.py:25
  310.5 61.9 %copy-start.5 = (f32[256,512]{0,1:T(8,128)S(1)}, f32[256,512]{0,1:T(8,128)}, u32[]{:S(2)}) copy-start(f32[256,512]{0,1:T(8,128)} %get-tuple-element.26) | copy-start | bytes 1572868
  375.8 219.1 %all-reduce.8.cloned.1.call-start = ((), (), s32[]{:S(2)}) async-start(), calls=%async_computation.5 | async-start | bytes 1048576 | tf_op jit(solution)/shard_map/psum | solution.py:96
  376.9 103.7 %copy-start.4 = (bf16[512,256]{1,0:T(8,128)(2,1)}, bf16[512,256]{1,0:T(8,128)(2,1)S(1)}, u32[]{:S(2)}) copy-start(bf16[512,256]{1,0:T(8,128)(2,1)S(1)} %copy.71) | copy-start | bytes 786436
  477.5 4.3 copy-start.6
  477.5 117.4 %copy-start.3 = (f32[256,256]{1,0:T(8,128)S(1)}, f32[256,256]{1,0:T(8,128)}, u32[]{:S(2)}) copy-start(f32[256,256]{1,0:T(8,128)} %param.16) | copy-start | bytes 786436
Sparse Core Ops, SparseCore 0:
  11.8 141.2 all-reduce.5
  156.0 58.1 all-gather.2
  240.7 69.7 all-reduce.9
  375.9 67.4 all-gather.4
  481.9 112.9 all-reduce.7
where the time goes:
time: 613 us; the launch traced here: 606 us
  waiting for transfers between devices  401 us (65%)
  local copies, waits for them, and re-layouts  67.8 us (11%)
  other arithmetic  57.9 us (9%)
  matrix products  46.8 us (8%)
  starting transfers between devices  17 us (3%)
  between operations  15.7 us (3%)
    all_gather x2, waiting for transfers between devices, neighbour(): lax.all_gather(slab_rows, 'ent', axis=0, tiled=True)  117 us
    psum x1, waiting for transfers between devices, shards(): totals = lax.psum(core_part, 'ent')  113 us
    psum x1, waiting for transfers between devices, shards(): lax.psum(jnp.einsum('ar,as->rs', factors, factors, preferred_element_type...  101 us
    psum x1, waiting for transfers between devices, shards(): numerator, system = lax.psum((forward_term + landed, system_part), 'rel')  69.7 us
    another operation x6, other arithmetic, shards(): factor_low = jnp.linalg.cholesky(system)  34 us
    unnamed x30, local copies, waits for them, and re-layouts  27.6 us
    another operation x3, other arithmetic, shards(): jax.scipy.linalg.cho_solve((factor_low, True), numerator.T)  19.7 us
  transfers between devices with their start and end apart: 7, of which 5 were waited for; matrix products, arithmetic and copies ran while one was open for 6% of the time, Pallas kernels for 0%

commit v1 on v0

--- a/solution.py
+++ b/solution.py
@@ -67,8 +67,11 @@
         precision=precise,
         preferred_element_type=jnp.float32,
     ).reshape(-1, rank_width)
-    gram_total = lax.psum(
-        jnp.einsum("ar,as->rs", factors, factors, preferred_element_type=jnp.float32), "ent"
+    gram_total = jnp.sum(
+        lax.all_gather(
+            jnp.einsum("ar,as->rs", factors, factors, preferred_element_type=jnp.float32), "ent"
+        ),
+        axis=0,
     )
     core_f32 = cores.astype(jnp.float32)
     system_part = jnp.einsum("kab,bc,kdc->ad", core_f32, gram_total, core_f32, precision=precise)

time: 613 us -> 578 us (0.943)
  waiting for transfers between devices: 401 us -> 360 us
    psum x1 -> x0, waiting for transfers between devices: 101 us -> none  [shards(): lax.psum(jnp.einsum('ar,as->rs', factors, factors, preferred_element_type...]
    all_to_all x1, waiting for transfers between devices: 0.01 us -> 63.9 us  [shards(): lax.all_to_all(backward_term, 'ent', split_axis=0, concat_axis=0, tiled=T...]
    unnamed x30 -> x34, local copies, waits for them, and re-layouts: 27.6 us -> 27.5 us
  transfers between devices with their start and end apart: 7 -> 7, of which waited for: 5 -> 5; matrix products, arithmetic and copies ran while one was open for 6% -> 7% of each run, Pallas kernels for 0% -> 0%
where the time goes in v1:
time: 578 us; the launch traced here: 571 us
  waiting for transfers between devices  360 us (62%)
  local copies, waits for them, and re-layouts  68.9 us (12%)
  other arithmetic  61.8 us (11%)
  matrix products  47.5 us (8%)
  starting transfers between devices  17 us (3%)
  between operations  15.7 us (3%)
    all_gather x2, waiting for transfers between devices, neighbour(): lax.all_gather(slab_rows, 'ent', axis=0, tiled=True)  113 us
    psum x1, waiting for transfers between devices, shards(): totals = lax.psum(core_part, 'ent')  113 us
    psum x1, waiting for transfers between devices, shards(): numerator, system = lax.psum((forward_term + landed, system_part), 'rel')  69.7 us
    all_to_all x1, waiting for transfers between devices, shards(): lax.all_to_all(backward_term, 'ent', split_axis=0, concat_axis=0, tiled=T...  63.9 us
    another operation x6, other arithmetic, shards(): factor_low = jnp.linalg.cholesky(system)  33.9 us
    unnamed x34, local copies, waits for them, and re-layouts  27.5 us
    another operation x3, other arithmetic, shards(): jax.scipy.linalg.cho_solve((factor_low, True), numerator.T)  19.7 us
    reshape x1, local copies, waits for them, and re-layouts, neighbour(): lax.all_gather(slab_rows, 'ent', axis=0, tiled=True)  12 us
  transfers between devices with their start and end apart: 7, of which 5 were waited for; matrix products, arithmetic and copies ran while one was open for 7% of the time, Pallas kernels for 0%

profile of v1, /device:TPU:1, one launch (start us, length us, event | category | flops | bytes accessed | tf_op | source)
XLA Modules:
  0.0 571.3 jit_solution(12468195734311456578)
XLA Ops:
  7.2 2.2 fusion.37
  9.5 0.7 all-gather.5.cloned.1.call-update
  10.2 1.3 copy.77
  11.5 8.6 %all-to-all-start = ((s32[32,1,1]{2,1,0:T(1,128)}), s32[32,1,1]{2,1,0:T(1,128)S(1)}, u32[]{:S(2)}, u32[]{:S(2)}) async-start(s32[32,1,1]{2,1,0:T(1,128)} %copy.77), calls=%async_computation | async-start | bytes 32768 | tf_op jit(solution)/shard_map/all_to_all | solution.py:22
  20.1 0.7 fusion.34
  20.8 2.8 gather_fusion.2
  23.6 5.4 convert_bitcast_fusion.1
  29.0 6.8 %copy.115 = bf16[8,8,128,256]{3,1,2,0:T(8,128)(2,1)} copy(bf16[8,8,128,256]{2,3,1,0:T(8,128)(2,1)} %bitcast.177) | data formatting | bytes 8388608
  35.9 3.6 convolution_convert_fusion
  39.5 1.1 copy.116
  40.6 3.2 convolution_bitcast_fusion
  43.9 7.5 %all-to-all-start.1 = ((f32[32,1,128,256]{3,2,1,0:T(8,128)}), f32[32,1,128,256]{3,2,1,0:T(8,128)}, u32[]{:S(2)}, u32[]{:S(2)}) async-start(f32[32,1,128,256]{3,2,1,0:T(8,128)} %convolution_bitcast_fusion), calls=%async_computation.1 | async-start | bytes 8388608 | tf_op jit(solution)/shard_map/all_to_all | solution.py:60
  51.4 0.5 all-reduce.7.cloned.1.call-start
  52.0 0.7 reduce.12
  52.7 63.9 %all-to-all-done.1 = f32[32,1,128,256]{3,2,1,0:T(8,128)} async-done(((f32[32,1,128,256]{3,2,1,0:T(8,128)}), f32[32,1,128,256]{3,2,1,0:T(8,128)}, u32[]{:S(2)}, u32[]{:S(2)}) %all-to-all-start.1) | async-done | bytes 4194336 | tf_op jit(solution)/shard_map/all_to_all | solution.py:60
  116.6 4.6 copy.117
  121.2 2.3 fusion.31
  123.5 1.4 reshape.241
  125.0 3.9 reduce_sum.9
  128.9 1.2 fusion.17
  130.2 1.2 fusion.19
  131.3 46.5 %all-gather.5.cloned.1.call-done = bf16[16384,256]{1,0:T(8,128)(2,1)} async-done(((bf16[512,256]{1,0:T(8,128)(2,1)}), bf16[16384,256]{1,0:T(8,128)(2,1)}) %all-gather.5.cloned.1.call-update) | async-done | bytes 8388624 | tf_op jit(solution)/shard_map/all_gather | solution.py:25
  177.8 5.5 gather_fusion
  183.3 4.4 gather_fusion.1
  187.6 5.5 convert_bitcast_fusion.2
  193.1 6.8 %copy.113 = bf16[8,8,128,256]{3,1,2,0:T(8,128)(2,1)} copy(bf16[8,8,128,256]{2,3,1,0:T(8,128)(2,1)} %bitcast.178) | data formatting | bytes 8388608
  199.9 3.0 convolution_convert_fusion.2
  203.1 0.5 convolution_bitcast_fusion.3
  203.6 1.1 fusion.4
  204.7 1.2 fusion.5
  206.1 69.7 %all-reduce.7.cloned.1.call-done = (f32[256,512]{0,1:T(8,128)}, f32[256,256]{0,1:T(8,128)}) async-done(((f32[256,512]{0,1:T(8,128)}, f32[256,256]{0,1:T(8,128)}), (f32[256,512]{0,1:T(8,128)}, f32[256,256]{0,1:T(8,128)})) %all-reduce.7.cloned.1.call-update) | async-done | bytes 786448 | tf_op jit(solution)/shard_map/psum | solution.py:81
  275.8 1.0 convert_add_fusion
  277.0 1.0 fusion.16
  278.0 11.7 %cholesky.50 = f32[128,128]{1,0:T(8,128)S(1)} custom-call(f32[128,128]{1,0:T(8,128)S(1)} %cholesky.118), custom_call_target="Cholesky" | custom-call | tf_op jit(solution)/shard_map/jit(cholesky)/cholesky | solution.py:83
  289.8 9.8 %custom-call.18 = f32[1,128,128]{1,2,0:T(8,128)S(1)} custom-call(f32[1,128,128]{2,1,0:T(8,128)S(1)} %get-tuple-element.35), custom_call_target="InvertDiagBlocksLowerTriangular" | custom-call | tf_op jit(solution)/shard_map/jit(cholesky)/cholesky | solution.py:83
  300.1 11.7 %cholesky.105 = f32[128,128]{1,0:T(8,128)S(1)} custom-call(f32[128,128]{1,0:T(8,128)S(1)} %convolution_subtract_fusion.2), custom_call_target="Cholesky" | custom-call | tf_op jit(solution)/shard_map/jit(cholesky)/cholesky | solution.py:83
  311.8 0.6 compare_reduce_fusion
  313.9 4.2 while.1
  314.1 0.6 fusion.70
  314.7 1.4 bitcast_dynamic-update-slice_fusion.2
  316.1 0.6 fusion.70
  316.7 1.4 bitcast_dynamic-update-slice_fusion.2
  318.1 19.7 %custom-call.19 = f32[2,128,128]{1,2,0:T(8,128)S(1)} custom-call(f32[2,128,128]{2,1,0:T(8,128)S(1)} %get-tuple-element.9), custom_call_target="InvertDiagBlocksLowerTriangular" | custom-call | tf_op jit(solution)/shard_map/jit(_cho_solve)/triangular_solve | solution.py:84
  337.8 0.4 fusion.6
  338.2 0.6 convolution_subtract_fusion.1
  338.8 0.4 fusion.25
  339.2 0.4 fusion.36
  339.6 0.4 convolution_subtract_fusion
  340.0 0.4 convolution_convert_fusion.3
  340.4 0.7 maximum_bitcast_fusion
  341.2 1.1 copy.90
  342.3 66.5 %all-gather.7.cloned.1.call-done = bf16[16384,256]{0,1:T(8,128)(2,1)} async-done(((bf16[512,256]{0,1:T(8,128)(2,1)}), bf16[16384,256]{0,1:T(8,128)(2,1)}) %all-gather.7.cloned.1.call-update) | async-done | bytes 8388624 | tf_op jit(solution)/shard_map/all_gather | solution.py:25
  408.8 12.0 %copy.111 = bf16[16384,256]{1,0:T(8,128)(2,1)} copy(bf16[16384,256]{0,1:T(8,128)(2,1)} %all-gather.7.cloned.1.call-done) | data formatting | bytes 16777216 | tf_op jit(solution)/shard_map/reshape | solution.py:25
  420.7 5.5 gather_fusion.3
  426.2 4.4 gather_fusion.4
  430.6 5.5 convert_bitcast_fusion
  436.0 6.8 %copy.118 = bf16[8,8,128,256]{3,1,2,0:T(8,128)(2,1)} copy(bf16[8,8,128,256]{2,3,1,0:T(8,128)(2,1)} %bitcast.179) | data formatting | bytes 8388608
  442.9 3.0 convolution_convert_fusion.1
  446.0 1.1 convolution_bitcast_fusion.1
  447.3 112.9 %all-reduce.5.cloned.1.call-done = f32[2,256,256]{1,2,0:T(8,128)} async-done(((f32[2,256,256]{1,2,0:T(8,128)}), f32[2,256,256]{1,2,0:T(8,128)}) %all-reduce.5.cloned.1.call-update) | async-done | bytes 524304 | tf_op jit(solution)/shard_map/psum | solution.py:99
  560.2 1.7 fusion.13
  561.9 0.6 convolution_multiply_fusion
  562.5 0.6 fusion.10
  563.2 1.4 fusion.8
  (60 shorter events, 1.7 us)
Async XLA Ops:
  7.2 16.4 %copy-start = (bf16[1,1,64,128,128]{4,3,2,1,0:T(8,128)(2,1)S(1)}, bf16[1,1,64,128,128]{4,3,2,1,0:T(8,128)(2,1)}, u32[]{:S(2)}) copy-start(bf16[1,1,64,128,128]{4,3,2,1,0:T(8,128)(2,1)} %param.9) | copy-start | bytes 6291460
  7.2 13.6 %copy-start.1 = (bf16[512,256]{1,0:T(8,128)(2,1)S(1)}, bf16[512,256]{1,0:T(8,128)(2,1)}, u32[]{:S(2)}) copy-start(bf16[512,256]{1,0:T(8,128)(2,1)} %param.14) | copy-start | bytes 786436
  7.2 117.8 %all-gather.9.cloned.1.call-start = ((), (), s32[]{:S(2)}) async-start(), calls=%async_computation.5 | async-start | bytes 8650752 | tf_op jit(solution)/shard_map/all_gather | solution.py:71
  9.4 168.4 %all-gather.5.cloned.1.call-start = ((), (), s32[]{:S(2)}) async-start(), calls=%async_computation.2 | async-start | bytes 8650752 | tf_op jit(solution)/shard_map/all_gather | solution.py:25
  11.5 32.3 %all-to-all-start = ((s32[32,1,1]{2,1,0:T(1,128)}), s32[32,1,1]{2,1,0:T(1,128)S(1)}, u32[]{:S(2)}, u32[]{:S(2)}) async-start(s32[32,1,1]{2,1,0:T(1,128)} %copy.77), calls=%async_computation | async-start | bytes 32768 | tf_op jit(solution)/shard_map/all_to_all | solution.py:22
  29.0 6.8 %copy-start.9 = (s32[1,1,64]{2,1,0:T(1,128)S(1)}, s32[1,1,64]{2,1,0:T(1,128)}, u32[]{:S(2)}) copy-start(s32[1,1,64]{2,1,0:T(1,128)} %param.10) | copy-start | bytes 772
  29.0 6.8 %copy-start.10 = (s32[1,1,64]{2,1,0:T(1,128)S(1)}, s32[1,1,64]{2,1,0:T(1,128)}, u32[]{:S(2)}) copy-start(s32[1,1,64]{2,1,0:T(1,128)} %param.11) | copy-start | bytes 772
  29.0 6.8 %copy-start.12 = (s32[1,1,64]{2,1,0:T(1,128)S(1)}, s32[1,1,64]{2,1,0:T(1,128)}, u32[]{:S(2)}) copy-start(s32[1,1,64]{2,1,0:T(1,128)} %param.12) | copy-start | bytes 772
  39.5 1.1 copy-start.2
  43.9 8.1 %copy-start.11 = (s32[1,1,32,1]{2,3,1,0:T(1,128)S(1)}, s32[1,1,32,1]{2,3,1,0:T(1,128)}, u32[]{:S(2)}) copy-start(s32[1,1,32,1]{2,3,1,0:T(1,128)} %param.13) | copy-start | bytes 388
  43.9 72.7 %all-to-all-start.1 = ((f32[32,1,128,256]{3,2,1,0:T(8,128)}), f32[32,1,128,256]{3,2,1,0:T(8,128)}, u32[]{:S(2)}, u32[]{:S(2)}) async-start(f32[32,1,128,256]{3,2,1,0:T(8,128)} %convolution_bitcast_fusion), calls=%async_computation.1 | async-start | bytes 8388608 | tf_op jit(solution)/shard_map/all_to_all | solution.py:60
  51.4 224.4 %all-reduce.7.cloned.1.call-start = ((), (), s32[]{:S(2)}) async-start(), calls=%async_computation.6 | async-start | bytes 1572864 | tf_op jit(solution)/shard_map/psum | solution.py:81
  199.9 3.2 copy-start.5
  199.9 4.8 copy-start.4
  205.9 202.9 %all-gather.7.cloned.1.call-start = ((), (), s32[]{:S(2)}) async-start(), calls=%async_computation.3 | async-start | bytes 8650752 | tf_op jit(solution)/shard_map/all_gather | solution.py:25
  275.8 61.9 %copy-start.7 = (f32[256,512]{0,1:T(8,128)S(1)}, f32[256,512]{0,1:T(8,128)}, u32[]{:S(2)}) copy-start(f32[256,512]{0,1:T(8,128)} %get-tuple-element.28) | copy-start | bytes 1572868
  341.1 219.1 %all-reduce.5.cloned.1.call-start = ((), (), s32[]{:S(2)}) async-start(), calls=%async_computation.4 | async-start | bytes 1048576 | tf_op jit(solution)/shard_map/psum | solution.py:99
  342.3 103.7 %copy-start.6 = (bf16[512,256]{1,0:T(8,128)(2,1)}, bf16[512,256]{1,0:T(8,128)(2,1)S(1)}, u32[]{:S(2)}) copy-start(bf16[512,256]{1,0:T(8,128)(2,1)S(1)} %copy.90) | copy-start | bytes 786436
  442.9 4.3 copy-start.8
  442.9 117.4 %copy-start.3 = (f32[256,256]{1,0:T(8,128)S(1)}, f32[256,256]{1,0:T(8,128)}, u32[]{:S(2)}) copy-start(f32[256,256]{1,0:T(8,128)} %param.16) | copy-start | bytes 786436
Sparse Core Ops, SparseCore 0:
  11.2 104.7 all-gather.8
  118.5 59.3 all-gather.4
  206.0 69.7 all-reduce.6
  341.3 67.4 all-gather.6
  447.3 112.9 all-reduce.4
